TPU v7x, 32 devices: a whole 2x2x4 slice. The times are simulated.
32 devices in a mesh: dp: 16 (over z, y, x), tensor: 2 (over core).
Axes of the slice: x: 2, y: 2, z: 4, core: 2. Of those that a mesh axis runs over, the one named last changes fastest.
Arguments:
- hidden_in: bfloat16 [32768, 768], P(('dp', 'tensor')), may hold values from -6 to 6
- out_grad: bfloat16 [32768, 768], P(('dp', 'tensor')), may hold values from -6 to 6
- seq_lengths: int32 [16, 8], P('dp'), may hold values from 1 to 1024, as said below
- attn_gain: bfloat16 [768], P('dp'), may hold values from 0.099609375 to 1.8984375
- attn_shift: bfloat16 [768], P('dp'), may hold values from -1.75 to 1.75
- mlp_gain: bfloat16 [768], P('dp'), may hold values from 0.099609375 to 1.8984375
- mlp_shift: bfloat16 [768], P('dp'), may hold values from -1.75 to 1.75
- qkv_weight: bfloat16 [768, 12, 192], P('dp', 'tensor'), may hold values from -0.21875 to 0.21875
- qkv_bias: bfloat16 [2304], P('dp'), may hold values from -1.75 to 1.75
- dense_weight: bfloat16 [768, 12, 64], P('dp', 'tensor'), may hold values from -0.875 to 0.875
- dense_bias: bfloat16 [768], P('dp'), may hold values from -1.75 to 1.75
- fc_weight: bfloat16 [768, 3072], P('dp', 'tensor'), may hold values from -0.21875 to 0.21875
- fc_bias: bfloat16 [3072], P('dp'), may hold values from -1.75 to 1.75
- proj_weight: bfloat16 [768, 3072], P('dp', 'tensor'), may hold values from -0.15625 to 0.15625
- proj_bias: bfloat16 [768], P('dp'), may hold values from -1.75 to 1.75
Outputs:
- block_out: bfloat16 [32768, 768], P(('dp', 'tensor'))
- input_grad: float32 [32768, 768], P(('dp', 'tensor'))
- attn_gain_grad: float32 [768], P(('dp', 'tensor'))
- attn_shift_grad: float32 [768], P(('dp', 'tensor'))
- mlp_gain_grad: float32 [768], P(('dp', 'tensor'))
- mlp_shift_grad: float32 [768], P(('dp', 'tensor'))
- qkv_weight_grad: float32 [768, 12, 192], P('dp', 'tensor')
- qkv_bias_grad: float32 [2304], P(('dp', 'tensor'))
- dense_weight_grad: float32 [768, 12, 64], P('dp', 'tensor')
- dense_bias_grad: float32 [768], P(('dp', 'tensor'))
- fc_weight_grad: float32 [768, 3072], P('dp', 'tensor')
- fc_bias_grad: float32 [3072], P(('dp', 'tensor'))
- proj_weight_grad: float32 [768, 3072], P('dp', 'tensor')
- proj_bias_grad: float32 [768], P(('dp', 'tensor'))
Inputs may be any that keep to these rules, and one draw needn't show every extreme that they name: `seq_lengths`: row g lists the 8 sequences of group g in order; they are all 1 or longer and sum to 2048. One sequence of each row has exactly 1024 rows and covers rows 1023 and 1024 of its group.
All inputs are finite; a program needn't handle non-finite values.
Results may differ from a plain program's by a relative error of at most 0.012.
Values may be sent and summed in bfloat16 or wider, within the bound.
A program may use at most 256 MiB of HBM per device.

v0:
```python
import jax
import jax.numpy as jnp
from jax import lax
from jax.sharding import PartitionSpec as P


def layout(lengths, group_rows):
    seq_index = jnp.arange(lengths.shape[0], dtype=jnp.int32)
    seq_ends = jnp.sum(
        jnp.where(seq_index[None, :] <= seq_index[:, None], lengths[None, :], 0), axis=1
    )
    starts = seq_ends - lengths
    row_index = jnp.arange(group_rows, dtype=jnp.int32)
    seg_ids = jnp.sum((row_index[:, None] >= seq_ends[None, :]).astype(jnp.int32), axis=1)
    owner_mask = seg_ids[:, None] == jnp.arange(lengths.shape[0], dtype=jnp.int32)[None, :]
    positions = row_index - jnp.sum(jnp.where(owner_mask, starts[None, :], 0), axis=1)
    return (seg_ids, positions)


def layer_norm(values, gain_vec, shift_vec):
    average = jnp.mean(values, axis=-1, keepdims=True)
    centred = values - average
    spread = jnp.mean(centred * centred, axis=-1, keepdims=True)
    return centred * lax.rsqrt(spread + 1e-05) * gain_vec + shift_vec


def rotary_tables(positions, head_dim):
    rot_dims = head_dim // 4
    half_rot = rot_dims // 2
    inv_freq = 10000.0 ** (-(jnp.arange(half_rot, dtype=jnp.float32) * 2.0 / rot_dims))
    angles = positions.astype(jnp.float32)[:, None] * inv_freq[None, :]
    angles = jnp.concatenate([angles, angles], axis=-1)
    return (jnp.cos(angles), jnp.sin(angles))


def rotate(vectors, cosine_table, sine_table):
    rot_dims = cosine_table.shape[-1]
    half_rot = rot_dims // 2
    rot_part = vectors[..., :rot_dims]
    turned = jnp.concatenate([-rot_part[..., half_rot:], rot_part[..., :half_rot]], axis=-1)
    result = rot_part * cosine_table[:, None, :] + turned * sine_table[:, None, :]
    return jnp.concatenate([result, vectors[..., rot_dims:]], axis=-1)


def exact_gelu(values):
    return jax.nn.gelu(values, approximate=False)


def body(
    hidden_in,
    out_grad,
    seq_lengths,
    attn_gain,
    attn_shift,
    mlp_gain,
    mlp_shift,
    qkv_weight,
    qkv_bias,
    dense_weight,
    dense_bias,
    fc_weight,
    fc_bias,
    proj_weight,
    proj_bias,
):
    tensor_index = lax.axis_index("tensor")
    tensor_count = lax.axis_size("tensor")
    local_rows = hidden_in.shape[0]
    group_rows = local_rows * tensor_count
    gathered = (
        lax.all_gather(qkv_weight, "dp", axis=0, tiled=True),
        lax.all_gather(dense_weight, "dp", axis=0, tiled=True),
        lax.all_gather(fc_weight, "dp", axis=0, tiled=True),
        lax.all_gather(proj_weight, "dp", axis=0, tiled=True),
        lax.all_gather(attn_gain, "dp", axis=0, tiled=True),
        lax.all_gather(attn_shift, "dp", axis=0, tiled=True),
        lax.all_gather(mlp_gain, "dp", axis=0, tiled=True),
        lax.all_gather(mlp_shift, "dp", axis=0, tiled=True),
        lax.all_gather(qkv_bias, "dp", axis=0, tiled=True),
        lax.all_gather(dense_bias, "dp", axis=0, tiled=True),
        lax.all_gather(fc_bias, "dp", axis=0, tiled=True),
        lax.all_gather(proj_bias, "dp", axis=0, tiled=True),
    )
    (
        w_qkv,
        w_dense,
        w_fc,
        w_proj,
        gain_attn,
        shift_attn,
        gain_mlp,
        shift_mlp,
        bias_qkv,
        bias_dense,
        bias_fc,
        bias_proj,
    ) = gathered
    model_width = w_qkv.shape[0]
    head_count = w_qkv.shape[1]
    triple_width = w_qkv.shape[2]
    head_dim = w_dense.shape[2]
    hidden_units = w_fc.shape[1]
    qkv_cols = head_count * triple_width
    attn_cols = head_count * head_dim
    my_bias_qkv = lax.dynamic_slice_in_dim(bias_qkv, tensor_index * qkv_cols, qkv_cols).astype(
        jnp.float32
    )
    my_bias_fc = lax.dynamic_slice_in_dim(
        bias_fc, tensor_index * hidden_units, hidden_units
    ).astype(jnp.float32)
    gain_attn_f = gain_attn.astype(jnp.float32)
    shift_attn_f = shift_attn.astype(jnp.float32)
    gain_mlp_f = gain_mlp.astype(jnp.float32)
    shift_mlp_f = shift_mlp.astype(jnp.float32)
    seg_ids, positions = layout(seq_lengths[0], group_rows)
    x_rows = hidden_in.astype(jnp.float32)

    def norms(values, gain_one, shift_one, gain_two, shift_two):
        return (layer_norm(values, gain_one, shift_one), layer_norm(values, gain_two, shift_two))

    (normed_one, normed_two), norm_back = jax.vjp(
        norms, x_rows, gain_attn_f, shift_attn_f, gain_mlp_f, shift_mlp_f
    )
    normed_attn, normed_mlp = (
        lax.all_gather(normed_one.astype(jnp.bfloat16), "tensor", axis=0, tiled=True),
        lax.all_gather(normed_two.astype(jnp.bfloat16), "tensor", axis=0, tiled=True),
    )
    merged_lin = (
        jnp.dot(
            normed_attn, w_qkv.reshape(model_width, qkv_cols), preferred_element_type=jnp.float32
        )
        + my_bias_qkv
    )
    merged_lin = merged_lin.reshape(group_rows, head_count, triple_width)
    cosine_table, sine_table = rotary_tables(positions, head_dim)

    def turn_pair(query_lin, key_lin):
        return (
            rotate(query_lin, cosine_table, sine_table),
            rotate(key_lin, cosine_table, sine_table),
        )

    (query_rot, key_rot), turn_back = jax.vjp(
        turn_pair, merged_lin[..., :head_dim], merged_lin[..., head_dim : 2 * head_dim]
    )
    query_low = query_rot.astype(jnp.bfloat16)
    key_low = key_rot.astype(jnp.bfloat16)
    value_low = merged_lin[..., 2 * head_dim :].astype(jnp.bfloat16)
    score_scale = head_dim ** (-0.5)
    block_rows = min(512, group_rows)
    block_count = group_rows // block_rows
    row_index = jnp.arange(group_rows, dtype=jnp.int32)

    def masked_scores(number):
        begin_row = number * block_rows
        end_row = begin_row + block_rows
        scores = (
            jnp.einsum(
                "qhd,khd->hqk",
                query_low[begin_row:end_row],
                key_low[:end_row],
                preferred_element_type=jnp.float32,
            )
            * score_scale
        )
        allowed = (row_index[None, :end_row] <= row_index[begin_row:end_row, None]) & (
            seg_ids[None, :end_row] == seg_ids[begin_row:end_row, None]
        )
        return jnp.where(allowed[None], scores, -1e30)

    head_blocks = []
    log_totals = []
    for number in range(block_count):
        end_row = (number + 1) * block_rows
        scores = masked_scores(number)
        peak_score = jnp.max(scores, axis=-1, keepdims=True)
        weights = jnp.exp(scores - peak_score)
        norm_total = jnp.sum(weights, axis=-1, keepdims=True)
        log_totals.append(peak_score + jnp.log(norm_total))
        prob_low = (weights / norm_total).astype(jnp.bfloat16)
        head_blocks.append(
            jnp.einsum(
                "hqk,khd->qhd", prob_low, value_low[:end_row], preferred_element_type=jnp.float32
            )
        )
    heads_flat = (
        jnp.concatenate(head_blocks, axis=0).astype(jnp.bfloat16).reshape(group_rows, attn_cols)
    )
    attn_part = jnp.einsum(
        "gc,dc->gd",
        heads_flat,
        w_dense.reshape(model_width, attn_cols),
        preferred_element_type=jnp.float32,
    )
    fc_pre = jnp.dot(normed_mlp, w_fc, preferred_element_type=jnp.float32) + my_bias_fc
    act_full, gelu_back = jax.vjp(exact_gelu, fc_pre)
    act_low = act_full.astype(jnp.bfloat16)
    mlp_part = jnp.einsum("gf,df->gd", act_low, w_proj, preferred_element_type=jnp.float32)
    branch_rows = lax.psum_scatter(
        (attn_part + mlp_part).astype(jnp.bfloat16), "tensor", scatter_dimension=0, tiled=True
    ).astype(jnp.float32)
    block_out = (
        x_rows + branch_rows + bias_dense.astype(jnp.float32) + bias_proj.astype(jnp.float32)
    ).astype(jnp.bfloat16)
    w_qkv, w_dense, w_fc, w_proj = (
        lax.all_gather(qkv_weight, "dp", axis=0, tiled=True),
        lax.all_gather(dense_weight, "dp", axis=0, tiled=True),
        lax.all_gather(fc_weight, "dp", axis=0, tiled=True),
        lax.all_gather(proj_weight, "dp", axis=0, tiled=True),
    )
    cot_all = lax.all_gather(out_grad, "tensor", axis=0, tiled=True)
    grad_act = jnp.dot(cot_all, w_proj, preferred_element_type=jnp.float32)
    grad_proj = jnp.einsum("gd,gf->df", cot_all, act_low, preferred_element_type=jnp.float32)
    grad_pre = gelu_back(grad_act)[0].astype(jnp.bfloat16)
    grad_fc = jnp.einsum("gd,gf->df", normed_mlp, grad_pre, preferred_element_type=jnp.float32)
    fc_bias_part = jnp.sum(grad_pre, axis=0, dtype=jnp.float32)
    grad_normed_mlp = jnp.einsum("gf,df->gd", grad_pre, w_fc, preferred_element_type=jnp.float32)
    dense_flat = w_dense.reshape(model_width, attn_cols)
    grad_heads = (
        jnp.dot(cot_all, dense_flat, preferred_element_type=jnp.float32)
        .astype(jnp.bfloat16)
        .reshape(group_rows, head_count, head_dim)
    )
    grad_dense = jnp.einsum(
        "gd,gc->dc", cot_all, heads_flat, preferred_element_type=jnp.float32
    ).reshape(model_width, head_count, head_dim)
    query_grads = []
    grad_key = jnp.zeros((group_rows, head_count, head_dim), jnp.float32)
    grad_value = jnp.zeros((group_rows, head_count, head_dim), jnp.float32)
    for number in range(block_count):
        begin_row = number * block_rows
        end_row = begin_row + block_rows
        probs = jnp.exp(masked_scores(number) - log_totals[number])
        heads_blk = grad_heads[begin_row:end_row]
        grad_probs = jnp.einsum(
            "qhd,khd->hqk", heads_blk, value_low[:end_row], preferred_element_type=jnp.float32
        )
        row_delta = jnp.sum(probs * grad_probs, axis=-1, keepdims=True)
        grad_scores = (probs * (grad_probs - row_delta)).astype(jnp.bfloat16)
        query_grads.append(
            jnp.einsum(
                "hqk,khd->qhd", grad_scores, key_low[:end_row], preferred_element_type=jnp.float32
            )
            * score_scale
        )
        grad_key = grad_key.at[:end_row].add(
            jnp.einsum(
                "hqk,qhd->khd",
                grad_scores,
                query_low[begin_row:end_row],
                preferred_element_type=jnp.float32,
            )
            * score_scale
        )
        grad_value = grad_value.at[:end_row].add(
            jnp.einsum(
                "hqk,qhd->khd",
                probs.astype(jnp.bfloat16),
                heads_blk,
                preferred_element_type=jnp.float32,
            )
        )
    grad_query = jnp.concatenate(query_grads, axis=0)
    grad_query_lin, grad_key_lin = turn_back((grad_query, grad_key))
    grad_merged = (
        jnp.concatenate([grad_query_lin, grad_key_lin, grad_value], axis=-1)
        .astype(jnp.bfloat16)
        .reshape(group_rows, qkv_cols)
    )
    grad_qkv = jnp.einsum(
        "gd,gc->dc", normed_attn, grad_merged, preferred_element_type=jnp.float32
    ).reshape(model_width, head_count, triple_width)
    qkv_bias_part = jnp.sum(grad_merged, axis=0, dtype=jnp.float32)
    grad_normed_attn = jnp.einsum(
        "gc,dc->gd",
        grad_merged,
        w_qkv.reshape(model_width, qkv_cols),
        preferred_element_type=jnp.float32,
    )
    cot_rows = out_grad.astype(jnp.float32)
    local_attn, local_mlp = (
        lax.psum_scatter(
            grad_normed_attn.astype(jnp.bfloat16), "tensor", scatter_dimension=0, tiled=True
        ).astype(jnp.float32),
        lax.psum_scatter(
            grad_normed_mlp.astype(jnp.bfloat16), "tensor", scatter_dimension=0, tiled=True
        ).astype(jnp.float32),
    )
    grad_x, grad_gain_attn, grad_shift_attn, grad_gain_mlp, grad_shift_mlp = norm_back(
        (local_attn, local_mlp)
    )
    input_grad = cot_rows + grad_x
    cot_sums = jnp.sum(cot_rows, axis=0)
    full_qkv_bias = lax.dynamic_update_slice_in_dim(
        jnp.zeros((qkv_cols * tensor_count,), jnp.float32),
        qkv_bias_part,
        tensor_index * qkv_cols,
        0,
    )
    full_fc_bias = lax.dynamic_update_slice_in_dim(
        jnp.zeros((hidden_units * tensor_count,), jnp.float32),
        fc_bias_part,
        tensor_index * hidden_units,
        0,
    )
    small_sums = (
        lax.psum_scatter(grad_gain_attn, ("dp", "tensor"), scatter_dimension=0, tiled=True),
        lax.psum_scatter(grad_shift_attn, ("dp", "tensor"), scatter_dimension=0, tiled=True),
        lax.psum_scatter(grad_gain_mlp, ("dp", "tensor"), scatter_dimension=0, tiled=True),
        lax.psum_scatter(grad_shift_mlp, ("dp", "tensor"), scatter_dimension=0, tiled=True),
        lax.psum_scatter(full_qkv_bias, ("dp", "tensor"), scatter_dimension=0, tiled=True),
        lax.psum_scatter(cot_sums, ("dp", "tensor"), scatter_dimension=0, tiled=True),
        lax.psum_scatter(full_fc_bias, ("dp", "tensor"), scatter_dimension=0, tiled=True),
    )
    large_sums = (
        lax.psum_scatter(grad_qkv, "dp", scatter_dimension=0, tiled=True),
        lax.psum_scatter(grad_dense, "dp", scatter_dimension=0, tiled=True),
        lax.psum_scatter(grad_fc, "dp", scatter_dimension=0, tiled=True),
        lax.psum_scatter(grad_proj, "dp", scatter_dimension=0, tiled=True),
    )
    return (
        block_out,
        input_grad,
        small_sums[0],
        small_sums[1],
        small_sums[2],
        small_sums[3],
        large_sums[0],
        small_sums[4],
        large_sums[1],
        small_sums[5],
        large_sums[2],
        small_sums[6],
        large_sums[3],
        small_sums[5],
    )


def solution(mesh):
    in_specs = (
        P(("dp", "tensor"), None),
        P(("dp", "tensor"), None),
        P("dp", None),
        P("dp"),
        P("dp"),
        P("dp"),
        P("dp"),
        P("dp", "tensor", None),
        P("dp"),
        P("dp", "tensor", None),
        P("dp"),
        P("dp", "tensor"),
        P("dp"),
        P("dp", "tensor"),
        P("dp"),
    )
    out_specs = (
        P(("dp", "tensor"), None),
        P(("dp", "tensor"), None),
        P(("dp", "tensor")),
        P(("dp", "tensor")),
        P(("dp", "tensor")),
        P(("dp", "tensor")),
        P("dp", "tensor", None),
        P(("dp", "tensor")),
        P("dp", "tensor", None),
        P(("dp", "tensor")),
        P("dp", "tensor"),
        P(("dp", "tensor")),
        P("dp", "tensor"),
        P(("dp", "tensor")),
    )
    return jax.shard_map(body, mesh=mesh, in_specs=in_specs, out_specs=out_specs, check_vma=False)
```

profile of v0, /device:TPU:0, one launch (start us, length us, event | category | flops | bytes accessed | tf_op | source)
XLA Modules:
  0.0 1065.3 jit_solution(10863352786644890494)
XLA Ops:
  18.7 79.0 %all-reduce.26 = (bf16[768]{0:T(1024)(128)(2,1)S(1)}, bf16[768]{0:T(1024)(128)(2,1)S(1)}, bf16[3072]{0:T(1024)(128)(2,1)S(1)}, bf16[768]{0:T(1024)(128)(2,1)S(1)...) all-reduce(bf16[768]{0:T(1024)(128)(2,1)S(1)} %dynamic-update-slice, ...), channel_id=1, replica_groups=mesh['dp'=16,'tensor'=2] {'dp'}, use_global_device_ids=true, to_apply=%add.14 | all-reduce | flops 9984 | bytes 39936
  105.8 44.1 %all_gather.54 = bf16[768,6,64]{2,0,1:T(8,128)(2,1)S(1)} all-gather(bf16[48,6,64]{2,0,1:T(8,128)(2,1)S(1)} %copy-done.50), channel_id=1, replica_groups=mesh['dp'=16,'tensor'=2] {'dp'}, dimensions={0}, use_global_device_ids=true | all-gather | bytes 626688 | tf_op jit(solution)/shard_map/all_gather | solution.py:72
  157.1 3.3 convolution_convert_fusion.1
  161.7 3.3 copy.54
  165.0 5.8 convolution_add_fusion
  178.1 4.0 multiply_reduce_fusion.3
  182.0 4.6 multiply_convert_fusion.4
  194.6 6.1 multiply_reduce_fusion.2
  200.7 6.3 multiply_convert_fusion.2
  211.7 8.4 fusion.153
  220.1 9.0 fusion.2
  229.1 12.9 %multiply_reduce_fusion.1 = (f32[6,512]{1,0:T(8,128)S(1)}, f32[6,512,1536]{2,1,0:T(8,128)}) fusion(f32[6,512,1536]{2,1,0:T(8,128)} %get-tuple-element.251, f32[6,512]{1,0:T(8,128)S(1)} %log_add_fusion.1, bf16[512,6,64]{0,2,1:T(8,128)(2,1)} %bitcast.137, bf16[2048,6,192]{0,2,1:T(8,128)(2,1)} %copy-done.9), kind=kOutput, calls=%fused_computation.10 | convolution fusion | flops 618132480 | bytes 39346176 | tf_op jit(solution)/shard_map/qhd,khd->hqk/dot_general | solution.py:235
  242.1 13.0 %multiply_convert_fusion.1 = bf16[6,512,1536]{2,1,0:T(8,128)(2,1)S(1)} fusion(f32[6,512,1536]{2,1,0:T(8,128)} %get-tuple-element.257, f32[6,512,1536]{2,1,0:T(8,128)} %get-tuple-element.251, f32[6,512]{1,0:T(8,128)S(1)} %get-tuple-element.256, f32[6,512]{1,0:T(8,128)S(1)} %log_add_fusion.1), kind=kLoop, calls=%fused_computation.9 | loop fusion | flops 18874368 | bytes 47210496 | tf_op jit(solution)/shard_map/convert_element_type | solution.py:239
  255.1 3.8 fusion.100
  260.8 10.7 %fusion.154 = (f32[6,512]{1,0:T(8,128)S(1)}, f32[6,512,2048]{2,1,0:T(8,128)}) fusion(bf16[512,6,64]{0,2,1:T(8,128)(2,1)S(1)} %copy-done.32, bf16[2048,6,16]{0,2,1:T(8,128)(2,1)S(1)} %get-tuple-element.213, bf16[2048,6,48]{0,2,1:T(8,128)(2,1)S(1)} %get-tuple-element.219, pred[512,2048]{1,0:T(8,128)(4,1)S(1)} %copy-done.38), kind=kOutput, calls=%fused_computation.255 | convolution fusion | flops 827323392 | bytes 28192768 | tf_op jit(solution)/shard_map/qhd,khd->hqk/dot_general | solution.py:158
  271.5 10.5 fusion
  282.0 16.2 %multiply_reduce_fusion = (f32[6,512]{1,0:T(8,128)S(1)}, f32[6,512,2048]{2,1,0:T(8,128)}) fusion(f32[6,512,2048]{2,1,0:T(8,128)} %get-tuple-element.253, f32[6,512]{1,0:T(8,128)S(1)} %log_add_fusion, bf16[512,6,64]{0,2,1:T(8,128)(2,1)S(1)} %bitcast.135, bf16[2048,6,192]{0,2,1:T(8,128)(2,1)} %copy-done.9), kind=kOutput, calls=%fused_computation.1 | convolution fusion | flops 824177664 | bytes 52322304 | tf_op jit(solution)/shard_map/qhd,khd->hqk/dot_general | solution.py:235
  298.2 17.0 %multiply_convert_fusion = bf16[6,512,2048]{2,1,0:T(8,128)(2,1)S(1)} fusion(f32[6,512,2048]{2,1,0:T(8,128)} %get-tuple-element.255, f32[6,512,2048]{2,1,0:T(8,128)} %get-tuple-element.253, f32[6,512]{1,0:T(8,128)S(1)} %get-tuple-element.254, f32[6,512]{1,0:T(8,128)S(1)} %log_add_fusion), kind=kLoop, calls=%fused_computation | loop fusion | flops 25165824 | bytes 62939136 | tf_op jit(solution)/shard_map/convert_element_type | solution.py:239
  315.2 4.4 copy-done.2
  319.7 6.1 fusion.99
  325.8 8.0 bitcast_add_fusion.2
  333.9 5.1 pad_maximum_fusion
  344.8 4.5 fusion.88
  349.4 6.4 fusion.68
  355.8 11.6 %bitcast_add_fusion.1 = bf16[2048,6,64]{0,2,1:T(8,128)(2,1)S(1)} fusion(f32[2048,6,64]{0,2,1:T(8,128)} %fusion.68, bf16[512,6,64]{0,2,1:T(8,128)(2,1)S(1)} %bitcast.136, f32[6,512,2048]{2,1,0:T(8,128)} %get-tuple-element.253, f32[6,512]{1,0:T(8,128)S(1)} %log_add_fusion), kind=kOutput, calls=%fused_computation.109 | convolution fusion | flops 819462144 | bytes 30289920 | tf_op jit(solution)/shard_map/hqk,qhd->khd/dot_general | solution.py:256
  375.9 6.6 bitcast_convert_fusion
  382.5 9.3 fusion.105
  392.5 34.9 %multiply_convert_fusion.3 = (bf16[2048,1536]{1,0:T(8,128)(2,1)}, f32[2048,1536]{1,0:T(8,128)}, f32[2048,1536]{1,0:T(8,128)}) fusion(f32[1536]{0:T(1024)S(1)} %copy-done.64, bf16[2048,768]{1,0:T(8,128)(2,1)} %all-gather.11.cloned.1.call-done, bf16[768,1536]{1,0:T(8,128)(2,1)} %all-gather.13.cloned.1.call-done), kind=kOutput, calls=%fused_computation.25 | convolution fusion | flops 5039456256 | bytes 36968448 | tf_op jit(solution)/shard_map/dot_general | solution.py:195
  427.3 17.0 %convert_reduce_fusion = (f32[1536]{0:T(1024)S(1)}, bf16[2048,1536]{1,0:T(8,128)(2,1)S(1)}) fusion(f32[2048,1536]{1,0:T(8,128)} %get-tuple-element.212, bf16[2048,768]{1,0:T(8,128)(2,1)} %all-gather.17.cloned.1.call-done, bf16[768,1536]{1,0:T(8,128)(2,1)} %all-gather.15.cloned.1.call-done, f32[2048,1536]{1,0:T(8,128)} %get-tuple-element.245, ...), kind=kOutput, calls=%fused_computation.19 | convolution fusion | flops 4885314048 | bytes 36974592 | tf_op jit(solution)/shard_map/dot_general | solution.py:212
  446.9 6.4 convolution_convert_fusion
  454.0 7.7 fusion.104
  461.8 4.1 fusion.103
  466.0 11.1 %fusion.106 = bf16[6,64,512]{2,1,0:T(8,128)(2,1)S(1)} fusion(f32[6,512,2048]{2,1,0:T(8,128)} %get-tuple-element.253, f32[6,512]{1,0:T(8,128)S(1)} %copy-done.60, f32[6,512]{1,0:T(8,128)S(1)} %copy-done.58, bf16[2048,6,192]{0,2,1:T(8,128)(2,1)} %copy-done.9), kind=kOutput, calls=%fused_computation.174 | convolution fusion | flops 824377344 | bytes 27156480 | tf_op jit(solution)/shard_map/hqk,khd->qhd/dot_general | solution.py:182
  477.2 7.3 fusion.155
  484.5 4.6 fusion.22
  489.1 3.3 fusion.80
  494.4 10.0 fusion.33
  504.5 9.8 fusion.156
  514.4 9.7 convolution_bitcast_fusion
  524.1 6.2 copy.69
  531.7 3.9 fusion.45
  535.6 3.3 fusion.50
  539.0 6.5 convert_reduce_fusion.5
  545.5 37.7 %all-reduce.25 = (f32[768]{0:T(1024)S(1)}, f32[768]{0:T(1024)S(1)}, f32[768]{0:T(1024)S(1)}, f32[768]{0:T(1024)S(1)}, f32[2304]{0:T(1024)S(1)}, /*index=5*/f32[768]{0:T(1024)S(1)}, f32[3072]{0:T(1024)S(1)}) all-reduce(f32[768]{0:T(1024)S(1)} %get-tuple-element.187, ...), channel_id=5, replica_groups=mesh['dp'=16,'tensor'=2] {'dp','tensor'}, use_global_device_ids=true, to_apply=%region_25.26.clone | all-reduce | flops 9216 | bytes 73728
  586.8 45.0 %reduce-scatter.18.cloned.1.call-done = f32[48,6,64]{2,0,1:T(8,128)} async-done(((f32[768,6,64]{2,0,1:T(8,128)}), f32[48,6,64]{2,0,1:T(8,128)}) %reduce-scatter.18.cloned.1.call-update) | async-done | bytes 73744 | tf_op jit(solution)/shard_map/reduce_scatter | solution.py:317
  631.8 141.7 %reduce-scatter.16.cloned.1.call-done = f32[48,6,192]{2,0,1:T(8,128)} async-done(((f32[768,6,192]{2,0,1:T(8,128)}), f32[48,6,192]{2,0,1:T(8,128)}) %reduce-scatter.16.cloned.1.call-update) | async-done | bytes 221200 | tf_op jit(solution)/shard_map/reduce_scatter | solution.py:316
  773.5 142.4 %reduce-scatter.20.cloned.1.call-done = f32[48,1536]{1,0:T(8,128)} async-done(((f32[768,1536]{1,0:T(8,128)}), f32[48,1536]{1,0:T(8,128)}) %reduce-scatter.20.cloned.1.call-update) | async-done | bytes 294928 | tf_op jit(solution)/shard_map/reduce_scatter | solution.py:318
  915.9 142.2 %reduce-scatter.22.cloned.1.call-done = f32[48,1536]{1,0:T(8,128)} async-done(((f32[768,1536]{1,0:T(8,128)}), f32[48,1536]{1,0:T(8,128)}) %reduce-scatter.22.cloned.1.call-update) | async-done | bytes 294928
  (298 shorter events, 73.2 us)
Async XLA Ops:
  7.2 92.2 %copy-start.3 = (bf16[1024,768]{1,0:T(8,128)(2,1)S(1)}, bf16[1024,768]{1,0:T(8,128)(2,1)}, u32[]{:S(2)}) copy-start(bf16[1024,768]{1,0:T(8,128)(2,1)} %param.35) | copy-start | bytes 4718596
  7.2 149.9 %all-gather.17.cloned.1.call-start = ((), (), s32[]{:S(2)}) async-start(), calls=%async_computation.13 | async-start | bytes 4718592 | tf_op jit(solution)/shard_map/all_gather | solution.py:211
  7.9 153.8 %all-gather.9.cloned.1.call-start = ((), (), s32[]{:S(2)}) async-start(), calls=%async_computation.8 | async-start | bytes 2506752 | tf_op jit(solution)/shard_map/all_gather | solution.py:71
  8.7 156.3 %all-gather.7.cloned.1.call-start = ((), (), s32[]{:S(2)}) async-start(), calls=%async_computation.7 | async-start | bytes 4718592 | tf_op jit(solution)/shard_map/all_gather | solution.py:125
  97.7 5.5 copy-start.46
  97.7 5.5 copy-start.48
  103.2 288.6 %all-gather.11.cloned.1.call-start = ((), (), s32[]{:S(2)}) async-start(), calls=%async_computation.9 | async-start | bytes 4718592 | tf_op jit(solution)/shard_map/all_gather | solution.py:126
  103.8 288.1 %all-gather.13.cloned.1.call-start = ((), (), s32[]{:S(2)}) async-start(), calls=%async_computation.10 | async-start | bytes 2506752 | tf_op jit(solution)/shard_map/all_gather | solution.py:73
  104.4 322.9 %all-gather.15.cloned.1.call-start = ((), (), s32[]{:S(2)}) async-start(), calls=%async_computation.11 | async-start | bytes 2506752 | tf_op jit(solution)/shard_map/all_gather | solution.py:74
  105.0 426.6 %reduce-scatter.14.cloned.1.call-start = ((), (), s32[]{:S(2)}) async-start(), calls=%async_computation.15 | async-start | bytes 4718592 | tf_op jit(solution)/shard_map/reduce_scatter | solution.py:282
  105.8 66.1 %copy-start.33 = (f32[2048,16]{0,1:T(8,128)}, f32[2048,16]{0,1:T(8,128)S(1)}, u32[]{:S(2)}) copy-start(f32[2048,16]{0,1:T(8,128)S(1)} %get-tuple-element.237) | copy-start | bytes 393220
  105.8 66.1 %copy-start.35 = (f32[2048,16]{0,1:T(8,128)}, f32[2048,16]{0,1:T(8,128)S(1)}, u32[]{:S(2)}) copy-start(f32[2048,16]{0,1:T(8,128)S(1)} %get-tuple-element.238) | copy-start | bytes 393220
  150.0 10.5 copy-start.18
  171.7 22.8 %copy-start.9 = (bf16[2048,6,192]{0,2,1:T(8,128)(2,1)}, bf16[2048,6,192]{0,2,1:T(8,128)(2,1)S(1)}, u32[]{:S(2)}) copy-start(bf16[2048,6,192]{0,2,1:T(8,128)(2,1)S(1)} %convert.33) | copy-start | bytes 14155780
  171.9 88.8 %copy-start.5 = (bf16[2048,6,48]{0,2,1:T(8,128)(2,1)}, bf16[2048,6,48]{0,2,1:T(8,128)(2,1)S(1)}, u32[]{:S(2)}) copy-start(bf16[2048,6,48]{0,2,1:T(8,128)(2,1)S(1)} %get-tuple-element.219) | copy-start | bytes 3538948
  174.8 7.2 copy-start.1
  191.9 8.8 copy-start
  194.5 6.1 copy-start.55
  211.7 8.4 copy-start.6
  260.7 10.8 %copy-start.8 = (f32[2048,6,64]{0,2,1:T(8,128)}, f32[2048,6,64]{0,2,1:T(8,128)S(1)}, u32[]{:S(2)}) copy-start(f32[2048,6,64]{0,2,1:T(8,128)S(1)} %fusion.61) | copy-start | bytes 9437188
  271.5 10.5 copy-start.57
  271.5 10.5 copy-start.21
  282.0 16.2 %copy-start.59 = (f32[6,512]{1,0:T(8,128)}, f32[6,512]{1,0:T(8,128)S(1)}, u32[]{:S(2)}) copy-start(f32[6,512]{1,0:T(8,128)S(1)} %fusion) | copy-start | bytes 36868
  325.8 8.1 copy-start.14
  325.8 8.1 copy-start.15
  325.8 8.1 copy-start.16
  325.8 18.1 %slice-start = ((s8[12582912]{0:T(1024)(128)(4,1)}), s8[4194304]{0:T(1024)(128)(4,1)S(1)}, s32[]{:S(2)}) async-start(s8[12582912]{0:T(1024)(128)(4,1)} %bitcast.128), calls=%async_computation.20 | async-start | bytes 8388608
  325.8 18.1 %slice-start.1 = ((s8[12582912]{0:T(1024)(128)(4,1)}), s8[4194304]{0:T(1024)(128)(4,1)S(1)}, s32[]{:S(2)}) async-start(s8[12582912]{0:T(1024)(128)(4,1)} %bitcast.128), calls=%async_computation.21 | async-start | bytes 8388608
  325.8 23.6 %slice-start.3 = ((s8[18874368]{0:T(1024)(128)(4,1)}), s8[4194304]{0:T(1024)(128)(4,1)S(1)}, s32[]{:S(2)}) async-start(s8[18874368]{0:T(1024)(128)(4,1)} %bitcast.130), calls=%async_computation.23 | async-start | bytes 8388608
  325.8 23.6 %slice-start.4 = ((s8[18874368]{0:T(1024)(128)(4,1)}), s8[4194304]{0:T(1024)(128)(4,1)S(1)}, s32[]{:S(2)}) async-start(s8[18874368]{0:T(1024)(128)(4,1)} %bitcast.130), calls=%async_computation.24 | async-start | bytes 8388608
  333.9 15.5 %slice-start.5 = ((s8[18874368]{0:T(1024)(128)(4,1)}), s8[4194304]{0:T(1024)(128)(4,1)S(1)}, s32[]{:S(2)}) async-start(s8[18874368]{0:T(1024)(128)(4,1)} %bitcast.130), calls=%async_computation.25 | async-start | bytes 8388608
  340.7 8.7 slice-start.6
  349.4 6.4 copy-start.22
  355.8 11.6 %copy-start.28 = (f32[2048,6,16]{0,2,1:T(8,128)S(1)}, f32[2048,6,16]{0,2,1:T(8,128)}, u32[]{:S(2)}) copy-start(f32[2048,6,16]{0,2,1:T(8,128)} %get-tuple-element.209) | copy-start | bytes 2359300
  391.8 139.8 %reduce-scatter.12.cloned.1.call-start = ((), (), s32[]{:S(2)}) async-start(), calls=%async_computation.14 | async-start | bytes 4718592 | tf_op jit(solution)/shard_map/reduce_scatter | solution.py:285
  427.3 19.6 %copy-start.68 = (bf16[768,1536]{1,0:T(8,128)(2,1)S(1)}, bf16[768,1536]{1,0:T(8,128)(2,1)}, u32[]{:S(2)}) copy-start(bf16[768,1536]{1,0:T(8,128)(2,1)} %all-gather.13.cloned.1.call-done) | copy-start | bytes 7077892
  453.3 8.5 copy-start.43
  453.4 8.5 copy-start.54
  453.4 85.6 %reduce-scatter.10.cloned.1.call-start = ((), (), s32[]{:S(2)}) async-start(), calls=%async_computation.12 | async-start | bytes 4718592 | tf_op jit(solution)/shard_map/reduce_scatter | solution.py:199
  466.0 11.1 %copy-start.67 = (bf16[768,1536]{1,0:T(8,128)(2,1)S(1)}, bf16[768,1536]{1,0:T(8,128)(2,1)}, u32[]{:S(2)}) copy-start(bf16[768,1536]{1,0:T(8,128)(2,1)} %all-gather.15.cloned.1.call-done) | copy-start | bytes 7077892
  477.1 7.3 copy-start.19
  477.1 7.3 copy-start.70
  489.1 142.7 %reduce-scatter.18.cloned.1.call-start = ((), (), s32[]{:S(2)}) async-start(), calls=%async_computation.17 | async-start | bytes 2506752 | tf_op jit(solution)/shard_map/reduce_scatter | solution.py:317
  494.4 279.2 %reduce-scatter.16.cloned.1.call-start = ((), (), s32[]{:S(2)}) async-start(), calls=%async_computation.16 | async-start | bytes 5013504 | tf_op jit(solution)/shard_map/reduce_scatter | solution.py:316
  504.4 411.5 %reduce-scatter.20.cloned.1.call-start = ((), (), s32[]{:S(2)}) async-start(), calls=%async_computation.18 | async-start | bytes 5013504 | tf_op jit(solution)/shard_map/reduce_scatter | solution.py:318
  514.4 543.8 %reduce-scatter.22.cloned.1.call-start = ((), (), s32[]{:S(2)}) async-start(), calls=%async_computation.19 | async-start | bytes 5013504
  530.3 5.3 copy-start.52
  583.9 474.8 %copy-start.71 = (f32[24]{0:T(128)}, f32[24]{0:T(128)S(1)}, u32[]{:S(2)}) copy-start(f32[24]{0:T(128)S(1)} %dynamic-slice.72) | copy-start | bytes 292
  (48 other events, 122.6 us)
Sparse Core Ops, SparseCore 0:
  9.6 14.8 all-gather.16
  27.1 64.0 all-gather.8
  103.4 7.9 all-gather.6
  112.8 13.2 all-gather.10
  128.8 64.0 all-gather.12
  195.5 61.1 all-gather.14
  391.9 8.2 reduce-scatter.13
  453.5 8.2 reduce-scatter.11
  489.2 7.7 reduce-scatter.9
  503.1 128.6 reduce-scatter.17
  637.6 135.9 reduce-scatter.15
  780.0 135.9 reduce-scatter.19
  921.7 136.4 reduce-scatter.21
where the time goes:
time: 1070 us
  waiting for transfers between devices  475 us (44%)
  matrix products  264 us (25%)
  blocking collectives  161 us (15%)
  other arithmetic  101 us (9%)
  local copies, waits for them, and re-layouts  46.5 us (4%)
  between operations  17.3 us (2%)
    unnamed x14, waiting for transfers between devices  145 us
    reduce_scatter x1, waiting for transfers between devices, body(): lax.psum_scatter(grad_fc, 'dp', scatter_dimension=0, tiled=True)  142 us
    reduce_scatter x1, waiting for transfers between devices, body(): lax.psum_scatter(grad_qkv, 'dp', scatter_dimension=0, tiled=True)  142 us
    unnamed x2, blocking collectives  117 us
    reduce_scatter x1, waiting for transfers between devices, body(): lax.psum_scatter(grad_dense, 'dp', scatter_dimension=0, tiled=True)  45 us
    all_gather x1, blocking collectives, body(): lax.all_gather(dense_weight, 'dp', axis=0, tiled=True)  44.1 us
    convert_element_type x4, other arithmetic, body(): grad_scores = (probs * (grad_probs - row_delta)).astype(jnp.bfloat16)  40.9 us
    dot_general x4, matrix products, body(): jnp.einsum('qhd,khd->hqk', heads_blk, value_low[:end_row], preferred_elem...  39.2 us
  transfers between devices with their start and end apart: 13, of which 4 were waited for; matrix products, arithmetic and copies ran while one was open for 37% of the time, Pallas kernels for 0%

commit v1 on v0

--- a/solution.py
+++ b/solution.py
@@ -2,6 +2,24 @@
 import jax.numpy as jnp
 from jax import lax
 from jax.sharding import PartitionSpec as P
+
+
+def gather_around(value, axis, dim):
+    ways, here, step = (lax.axis_size(axis), lax.axis_index(axis), value.shape[dim])
+    dims = [n * ways if d == dim else n for d, n in enumerate(value.shape)]
+    full = lax.dynamic_update_slice_in_dim(
+        jnp.zeros(dims, value.dtype), value, here * step, axis=dim
+    )
+    going_up = going_down = value
+    for far in range(1, ways // 2 + 1):
+        going_up = lax.ppermute(going_up, axis, [(d, (d + 1) % ways) for d in range(ways)])
+        full = lax.dynamic_update_slice_in_dim(full, going_up, (here - far) % ways * step, axis=dim)
+        if 2 * far < ways:
+            going_down = lax.ppermute(going_down, axis, [(d, (d - 1) % ways) for d in range(ways)])
+            full = lax.dynamic_update_slice_in_dim(
+                full, going_down, (here + far) % ways * step, axis=dim
+            )
+    return full
 
 
 def layout(lengths, group_rows):
@@ -69,7 +87,7 @@
     group_rows = local_rows * tensor_count
     gathered = (
         lax.all_gather(qkv_weight, "dp", axis=0, tiled=True),
-        lax.all_gather(dense_weight, "dp", axis=0, tiled=True),
+        gather_around(dense_weight, "dp", 0),
         lax.all_gather(fc_weight, "dp", axis=0, tiled=True),
         lax.all_gather(proj_weight, "dp", axis=0, tiled=True),
         lax.all_gather(attn_gain, "dp", axis=0, tiled=True),

time: 1070 us -> 1150 us (1.075)
  starting transfers between devices: 0.52 us -> 41.1 us
  local copies, waits for them, and re-layouts: 46.5 us -> 73.3 us
    ppermute x0 -> x15, starting transfers between devices: none -> 40.6 us  [the longest x7 39 us: gather_around(): lax.ppermute(going_down, axis, [(d, (d - 1) % ways) for d in range(ways)])]
    dynamic_update_slice x0 -> x16, local copies, waits for them, and re-layouts: none -> 20.5 us  [the longest x8 10.2 us: gather_around(): lax.dynamic_update_slice_in_dim(full, going_up, (here - far) % ways * ste...]
    ppermute x0 -> x15, waiting for transfers between devices: none -> 11.7 us  [the longest x8 9.52 us: gather_around(): lax.ppermute(going_up, axis, [(d, (d + 1) % ways) for d in range(ways)])]
    unnamed x188 -> x197, local copies, waits for them, and re-layouts: 34.7 us -> 35 us
  transfers between devices with their start and end apart: 13 -> 28, of which waited for: 4 -> 12; matrix products, arithmetic and copies ran while one was open for 37% -> 37% of each run, Pallas kernels for 0% -> 0%
where the time goes in v1:
time: 1150 us
  waiting for transfers between devices  485 us (42%)
  matrix products  263 us (23%)
  blocking collectives  165 us (14%)
  other arithmetic  101 us (9%)
  local copies, waits for them, and re-layouts  73.3 us (6%)
  starting transfers between devices  41.1 us (4%)
  between operations  17.9 us (2%)
    unnamed x14, waiting for transfers between devices  144 us
    reduce_scatter x1, waiting for transfers between devices, body(): lax.psum_scatter(grad_fc, 'dp', scatter_dimension=0, tiled=True)  142 us
    reduce_scatter x1, waiting for transfers between devices, body(): lax.psum_scatter(grad_qkv, 'dp', scatter_dimension=0, tiled=True)  142 us
    unnamed x2, blocking collectives  120 us
    reduce_scatter x1, waiting for transfers between devices, body(): lax.psum_scatter(grad_dense, 'dp', scatter_dimension=0, tiled=True)  45.5 us
    all_gather x1, blocking collectives, body(): lax.all_gather(dense_weight, 'dp', axis=0, tiled=True)  44.9 us
    convert_element_type x4, other arithmetic, body(): grad_scores = (probs * (grad_probs - row_delta)).astype(jnp.bfloat16)  40.4 us
    dot_general x4, matrix products, body(): jnp.einsum('qhd,khd->hqk', heads_blk, value_low[:end_row], preferred_elem...  39.2 us
  transfers between devices with their start and end apart: 28, of which 12 were waited for; matrix products, arithmetic and copies ran while one was open for 37% of the time, Pallas kernels for 0%

profile of v1, /device:TPU:0, one launch (start us, length us, event | category | flops | bytes accessed | tf_op | source)
XLA Modules:
  0.0 1146.4 jit_solution(8605995186709545158)
XLA Ops:
  18.7 79.0 %all-reduce.26 = (bf16[768]{0:T(1024)(128)(2,1)S(1)}, bf16[768]{0:T(1024)(128)(2,1)S(1)}, bf16[3072]{0:T(1024)(128)(2,1)S(1)}, bf16[768]{0:T(1024)(128)(2,1)S(1)...) all-reduce(bf16[768]{0:T(1024)(128)(2,1)S(1)} %dynamic-update-slice, ...), channel_id=1, replica_groups=mesh['dp'=16,'tensor'=2] {'dp'}, use_global_device_ids=true, to_apply=%add.14 | all-reduce | flops 9984 | bytes 39936
  104.5 5.6 collective-permute-start.1
  114.3 44.9 %all_gather.62 = bf16[768,6,64]{2,0,1:T(8,128)(2,1)S(1)} all-gather(bf16[48,6,64]{2,0,1:T(8,128)(2,1)S(1)} %copy-done.40), channel_id=1, replica_groups=mesh['dp'=16,'tensor'=2] {'dp'}, dimensions={0}, use_global_device_ids=true | all-gather | bytes 626688 | tf_op jit(solution)/shard_map/all_gather | solution.py:225
  160.7 4.2 collective-permute-start.3
  167.3 5.9 collective-permute-start.5
  176.5 5.6 collective-permute-start.7
  185.5 5.6 collective-permute-start.9
  194.5 6.1 collective-permute-start.11
  202.5 6.1 collective-permute-start.13
  244.8 5.8 convolution_add_fusion
  257.8 4.1 multiply_reduce_fusion.3
  261.9 4.6 multiply_convert_fusion.4
  274.4 6.0 multiply_reduce_fusion.2
  280.4 6.2 multiply_convert_fusion.2
  291.3 8.4 fusion.153
  299.7 9.0 fusion.2
  308.8 13.0 %multiply_reduce_fusion.1 = (f32[6,512]{1,0:T(8,128)S(1)}, f32[6,512,1536]{2,1,0:T(8,128)}) fusion(f32[6,512,1536]{2,1,0:T(8,128)} %get-tuple-element.251, f32[6,512]{1,0:T(8,128)S(1)} %log_add_fusion.1, bf16[512,6,64]{0,2,1:T(8,128)(2,1)} %bitcast.137, bf16[2048,6,192]{0,2,1:T(8,128)(2,1)} %copy-done.9), kind=kOutput, calls=%fused_computation.10 | convolution fusion | flops 618132480 | bytes 39346176 | tf_op jit(solution)/shard_map/qhd,khd->hqk/dot_general | solution.py:253
  321.8 12.9 %multiply_convert_fusion.1 = bf16[6,512,1536]{2,1,0:T(8,128)(2,1)S(1)} fusion(f32[6,512,1536]{2,1,0:T(8,128)} %get-tuple-element.257, f32[6,512,1536]{2,1,0:T(8,128)} %get-tuple-element.251, f32[6,512]{1,0:T(8,128)S(1)} %get-tuple-element.256, f32[6,512]{1,0:T(8,128)S(1)} %log_add_fusion.1), kind=kLoop, calls=%fused_computation.9 | loop fusion | flops 18874368 | bytes 47210496 | tf_op jit(solution)/shard_map/convert_element_type | solution.py:257
  340.4 10.5 fusion.154
  350.9 10.5 fusion
  361.4 16.1 %multiply_reduce_fusion = (f32[6,512]{1,0:T(8,128)S(1)}, f32[6,512,2048]{2,1,0:T(8,128)}) fusion(f32[6,512,2048]{2,1,0:T(8,128)} %get-tuple-element.253, f32[6,512]{1,0:T(8,128)S(1)} %log_add_fusion, bf16[512,6,64]{0,2,1:T(8,128)(2,1)S(1)} %bitcast.135, bf16[2048,6,192]{0,2,1:T(8,128)(2,1)} %copy-done.9), kind=kOutput, calls=%fused_computation.1 | convolution fusion | flops 824177664 | bytes 52322304 | tf_op jit(solution)/shard_map/qhd,khd->hqk/dot_general | solution.py:253
  377.5 16.7 %multiply_convert_fusion = bf16[6,512,2048]{2,1,0:T(8,128)(2,1)S(1)} fusion(f32[6,512,2048]{2,1,0:T(8,128)} %get-tuple-element.255, f32[6,512,2048]{2,1,0:T(8,128)} %get-tuple-element.253, f32[6,512]{1,0:T(8,128)S(1)} %get-tuple-element.254, f32[6,512]{1,0:T(8,128)S(1)} %log_add_fusion), kind=kLoop, calls=%fused_computation | loop fusion | flops 25165824 | bytes 62939136 | tf_op jit(solution)/shard_map/convert_element_type | solution.py:257
  394.3 4.5 copy-done.2
  398.8 6.1 fusion.99
  404.9 8.0 bitcast_add_fusion.2
  413.0 5.0 pad_maximum_fusion
  423.8 4.5 fusion.88
  428.4 6.4 fusion.68
  434.8 11.6 %bitcast_add_fusion.1 = bf16[2048,6,64]{0,2,1:T(8,128)(2,1)S(1)} fusion(f32[2048,6,64]{0,2,1:T(8,128)} %fusion.68, bf16[512,6,64]{0,2,1:T(8,128)(2,1)S(1)} %bitcast.136, f32[6,512,2048]{2,1,0:T(8,128)} %get-tuple-element.253, f32[6,512]{1,0:T(8,128)S(1)} %log_add_fusion), kind=kOutput, calls=%fused_computation.109 | convolution fusion | flops 819462144 | bytes 30289920 | tf_op jit(solution)/shard_map/hqk,qhd->khd/dot_general | solution.py:274
  455.1 6.6 bitcast_convert_fusion
  461.7 9.3 fusion.105
  471.6 34.8 %multiply_convert_fusion.3 = (bf16[2048,1536]{1,0:T(8,128)(2,1)}, f32[2048,1536]{1,0:T(8,128)}, f32[2048,1536]{1,0:T(8,128)}) fusion(f32[1536]{0:T(1024)S(1)} %copy-done.68, bf16[2048,768]{1,0:T(8,128)(2,1)} %all-gather.11.cloned.1.call-done, bf16[768,1536]{1,0:T(8,128)(2,1)} %all-gather.13.cloned.1.call-done), kind=kOutput, calls=%fused_computation.25 | convolution fusion | flops 5039456256 | bytes 36968448 | tf_op jit(solution)/shard_map/dot_general | solution.py:213
  506.5 17.0 %convert_reduce_fusion = (f32[1536]{0:T(1024)S(1)}, bf16[2048,1536]{1,0:T(8,128)(2,1)S(1)}) fusion(f32[2048,1536]{1,0:T(8,128)} %get-tuple-element.212, bf16[2048,768]{1,0:T(8,128)(2,1)} %all-gather.17.cloned.1.call-done, bf16[768,1536]{1,0:T(8,128)(2,1)} %all-gather.15.cloned.1.call-done, f32[2048,1536]{1,0:T(8,128)} %get-tuple-element.245, ...), kind=kOutput, calls=%fused_computation.19 | convolution fusion | flops 4885314048 | bytes 36974592 | tf_op jit(solution)/shard_map/dot_general | solution.py:230
  526.2 6.4 convolution_convert_fusion
  533.3 6.3 fusion.104
  539.7 4.7 fusion.103
  544.4 11.2 fusion.106
  555.6 7.3 fusion.155
  572.0 10.5 fusion.33
  582.6 10.0 fusion.156
  592.7 9.8 convolution_bitcast_fusion
  602.5 6.2 copy.133
  617.4 6.5 convert_reduce_fusion.5
  623.9 40.8 %all-reduce.25 = (f32[768]{0:T(1024)S(1)}, f32[768]{0:T(1024)S(1)}, f32[768]{0:T(1024)S(1)}, f32[768]{0:T(1024)S(1)}, f32[2304]{0:T(1024)S(1)}, /*index=5*/f32[768]{0:T(1024)S(1)}, f32[3072]{0:T(1024)S(1)}) all-reduce(f32[768]{0:T(1024)S(1)} %get-tuple-element.187, ...), channel_id=5, replica_groups=mesh['dp'=16,'tensor'=2] {'dp','tensor'}, use_global_device_ids=true, to_apply=%region_25.26.clone | all-reduce | flops 9216 | bytes 73728
  668.3 45.5 %reduce-scatter.18.cloned.1.call-done = f32[48,6,64]{2,0,1:T(8,128)} async-done(((f32[768,6,64]{2,0,1:T(8,128)}), f32[48,6,64]{2,0,1:T(8,128)}) %reduce-scatter.18.cloned.1.call-update) | async-done | bytes 73744 | tf_op jit(solution)/shard_map/reduce_scatter | solution.py:335
  713.8 141.7 %reduce-scatter.16.cloned.1.call-done = f32[48,6,192]{2,0,1:T(8,128)} async-done(((f32[768,6,192]{2,0,1:T(8,128)}), f32[48,6,192]{2,0,1:T(8,128)}) %reduce-scatter.16.cloned.1.call-update) | async-done | bytes 221200 | tf_op jit(solution)/shard_map/reduce_scatter | solution.py:334
  855.5 142.2 %reduce-scatter.20.cloned.1.call-done = f32[48,1536]{1,0:T(8,128)} async-done(((f32[768,1536]{1,0:T(8,128)}), f32[48,1536]{1,0:T(8,128)}) %reduce-scatter.20.cloned.1.call-update) | async-done | bytes 294928 | tf_op jit(solution)/shard_map/reduce_scatter | solution.py:336
  997.7 141.4 %reduce-scatter.22.cloned.1.call-done = f32[48,1536]{1,0:T(8,128)} async-done(((f32[768,1536]{1,0:T(8,128)}), f32[48,1536]{1,0:T(8,128)}) %reduce-scatter.22.cloned.1.call-update) | async-done | bytes 294928
  (369 shorter events, 137.6 us)
Async XLA Ops:
  7.2 92.2 %copy-start.3 = (bf16[1024,768]{1,0:T(8,128)(2,1)S(1)}, bf16[1024,768]{1,0:T(8,128)(2,1)}, u32[]{:S(2)}) copy-start(bf16[1024,768]{1,0:T(8,128)(2,1)} %param.35) | copy-start | bytes 4718596
  7.2 229.6 %all-gather.17.cloned.1.call-start = ((), (), s32[]{:S(2)}) async-start(), calls=%async_computation.13 | async-start | bytes 4718592 | tf_op jit(solution)/shard_map/all_gather | solution.py:229
  7.9 233.7 %all-gather.9.cloned.1.call-start = ((), (), s32[]{:S(2)}) async-start(), calls=%async_computation.8 | async-start | bytes 2506752 | tf_op jit(solution)/shard_map/all_gather | solution.py:89
  8.7 236.1 %all-gather.7.cloned.1.call-start = ((), (), s32[]{:S(2)}) async-start(), calls=%async_computation.7 | async-start | bytes 4718592 | tf_op jit(solution)/shard_map/all_gather | solution.py:143
  103.2 367.8 %all-gather.11.cloned.1.call-start = ((), (), s32[]{:S(2)}) async-start(), calls=%async_computation.9 | async-start | bytes 4718592 | tf_op jit(solution)/shard_map/all_gather | solution.py:144
  103.8 367.2 %all-gather.13.cloned.1.call-start = ((), (), s32[]{:S(2)}) async-start(), calls=%async_computation.10 | async-start | bytes 2506752 | tf_op jit(solution)/shard_map/all_gather | solution.py:91
  104.4 402.1 %all-gather.15.cloned.1.call-start = ((), (), s32[]{:S(2)}) async-start(), calls=%async_computation.11 | async-start | bytes 2506752 | tf_op jit(solution)/shard_map/all_gather | solution.py:92
  104.5 54.8 %collective-permute-start = (bf16[48,6,64]{2,0,1:T(8,128)(2,1)S(1)}, bf16[48,6,64]{2,0,1:T(8,128)(2,1)S(1)}, u32[]{:S(2)}, u32[]{:S(2)}) collective-permute-start(bf16[48,6,64]{2,0,1:T(8,128)(2,1)S(1)} %copy-done.40), channel_id=1, source_target_pairs={{0,2},{2,4},{4,6},{6,8},{8,10},{10,12},{12,14},{14,16},{16,18},{18... | collective-permute-start | bytes 110600 | tf_op jit(solution)/shard_map/ppermute | solution.py:15
  104.5 56.2 %collective-permute-start.1 = (bf16[48,6,64]{2,0,1:T(8,128)(2,1)S(1)}, bf16[48,6,64]{2,0,1:T(8,128)(2,1)S(1)}, u32[]{:S(2)}, u32[]{:S(2)}) collective-permute-start(bf16[48,6,64]{2,0,1:T(8,128)(2,1)S(1)} %copy-done.40), channel_id=1, source_target_pairs={{0,30},{2,0},{4,2},{6,4},{8,6},{10,8},{12,10},{14,12},{16,14},{18,... | collective-permute-start | bytes 110600 | tf_op jit(solution)/shard_map/ppermute | solution.py:18
  110.2 499.8 %reduce-scatter.14.cloned.1.call-start = ((), (), s32[]{:S(2)}) async-start(), calls=%async_computation.15 | async-start | bytes 4718592 | tf_op jit(solution)/shard_map/reduce_scatter | solution.py:300
  159.2 8.1 collective-permute-start.2
  160.7 6.6 collective-permute-start.3
  167.3 7.9 collective-permute-start.4
  167.3 9.2 collective-permute-start.5
  175.2 9.3 collective-permute-start.6
  176.5 9.0 collective-permute-start.7
  184.6 8.4 collective-permute-start.8
  185.5 8.9 collective-permute-start.9
  192.9 8.1 collective-permute-start.10
  193.2 58.6 %copy-start.31 = (f32[2048,16]{0,1:T(8,128)}, f32[2048,16]{0,1:T(8,128)S(1)}, u32[]{:S(2)}) copy-start(f32[2048,16]{0,1:T(8,128)S(1)} %get-tuple-element.237) | copy-start | bytes 393220
  193.2 58.6 %copy-start.33 = (f32[2048,16]{0,1:T(8,128)}, f32[2048,16]{0,1:T(8,128)S(1)}, u32[]{:S(2)}) copy-start(f32[2048,16]{0,1:T(8,128)S(1)} %get-tuple-element.238) | copy-start | bytes 393220
  194.5 14.9 %copy-start.51 = (bf16[48,6,64]{2,0,1:T(8,128)(2,1)}, bf16[48,6,64]{2,0,1:T(8,128)(2,1)S(1)}, u32[]{:S(2)}) copy-start(bf16[48,6,64]{2,0,1:T(8,128)(2,1)S(1)} %collective-permute-done.9) | copy-start | bytes 110596
  194.5 8.1 collective-permute-start.11
  201.0 8.1 collective-permute-start.12
  202.5 30.4 %collective-permute-start.13 = (bf16[48,6,64]{2,0,1:T(8,128)(2,1)}, bf16[48,6,64]{2,0,1:T(8,128)(2,1)}, u32[]{:S(2)}, u32[]{:S(2)}) collective-permute-start(bf16[48,6,64]{2,0,1:T(8,128)(2,1)} %collective-permute-done.11), channel_id=1, source_target_pairs={{0,30},{2,0},{4,2},{6,4},{8,6},{10,8},{12,10},{14,12},{16,14},{18,... | collective-permute-start | bytes 110600 | tf_op jit(solution)/shard_map/ppermute | solution.py:18
  209.0 26.3 %collective-permute-start.14 = (bf16[48,6,64]{2,0,1:T(8,128)(2,1)}, bf16[48,6,64]{2,0,1:T(8,128)(2,1)}, u32[]{:S(2)}, u32[]{:S(2)}) collective-permute-start(bf16[48,6,64]{2,0,1:T(8,128)(2,1)} %collective-permute-done.12), channel_id=1, source_target_pairs={{0,2},{2,4},{4,6},{6,8},{8,10},{10,12},{12,14},{14,16},{16,18},{18... | collective-permute-start | bytes 110600 | tf_op jit(solution)/shard_map/ppermute | solution.py:15
  209.5 15.5 %copy-start.52 = (bf16[48,6,64]{2,0,1:T(8,128)(2,1)S(1)}, bf16[48,6,64]{2,0,1:T(8,128)(2,1)}, u32[]{:S(2)}) copy-start(bf16[48,6,64]{2,0,1:T(8,128)(2,1)} %copy-done.51) | copy-start | bytes 110596
  210.5 16.0 %copy-start.54 = (bf16[48,6,64]{2,0,1:T(8,128)(2,1)S(1)}, bf16[48,6,64]{2,0,1:T(8,128)(2,1)}, u32[]{:S(2)}) copy-start(bf16[48,6,64]{2,0,1:T(8,128)(2,1)} %copy-done.53) | copy-start | bytes 110596
  251.5 22.9 %copy-start.9 = (bf16[2048,6,192]{0,2,1:T(8,128)(2,1)}, bf16[2048,6,192]{0,2,1:T(8,128)(2,1)S(1)}, u32[]{:S(2)}) copy-start(bf16[2048,6,192]{0,2,1:T(8,128)(2,1)S(1)} %convert.33) | copy-start | bytes 14155780
  251.7 88.6 %copy-start.5 = (bf16[2048,6,48]{0,2,1:T(8,128)(2,1)}, bf16[2048,6,48]{0,2,1:T(8,128)(2,1)S(1)}, u32[]{:S(2)}) copy-start(bf16[2048,6,48]{0,2,1:T(8,128)(2,1)S(1)} %get-tuple-element.219) | copy-start | bytes 3538948
  340.3 10.6 copy-start.8
  350.9 10.5 copy-start.19
  361.4 16.1 %copy-start.63 = (f32[6,512]{1,0:T(8,128)}, f32[6,512]{1,0:T(8,128)S(1)}, u32[]{:S(2)}) copy-start(f32[6,512]{1,0:T(8,128)S(1)} %fusion) | copy-start | bytes 36868
  404.8 18.0 %slice-start = ((s8[12582912]{0:T(1024)(128)(4,1)}), s8[4194304]{0:T(1024)(128)(4,1)S(1)}, s32[]{:S(2)}) async-start(s8[12582912]{0:T(1024)(128)(4,1)} %bitcast.128), calls=%async_computation.20 | async-start | bytes 8388608
  404.8 18.0 %slice-start.1 = ((s8[12582912]{0:T(1024)(128)(4,1)}), s8[4194304]{0:T(1024)(128)(4,1)S(1)}, s32[]{:S(2)}) async-start(s8[12582912]{0:T(1024)(128)(4,1)} %bitcast.128), calls=%async_computation.21 | async-start | bytes 8388608
  404.8 23.5 %slice-start.3 = ((s8[18874368]{0:T(1024)(128)(4,1)}), s8[4194304]{0:T(1024)(128)(4,1)S(1)}, s32[]{:S(2)}) async-start(s8[18874368]{0:T(1024)(128)(4,1)} %bitcast.130), calls=%async_computation.23 | async-start | bytes 8388608
  404.9 23.5 %slice-start.4 = ((s8[18874368]{0:T(1024)(128)(4,1)}), s8[4194304]{0:T(1024)(128)(4,1)S(1)}, s32[]{:S(2)}) async-start(s8[18874368]{0:T(1024)(128)(4,1)} %bitcast.130), calls=%async_computation.24 | async-start | bytes 8388608
  413.0 15.4 %slice-start.5 = ((s8[18874368]{0:T(1024)(128)(4,1)}), s8[4194304]{0:T(1024)(128)(4,1)S(1)}, s32[]{:S(2)}) async-start(s8[18874368]{0:T(1024)(128)(4,1)} %bitcast.130), calls=%async_computation.25 | async-start | bytes 8388608
  434.8 11.6 %copy-start.26 = (f32[2048,6,16]{0,2,1:T(8,128)S(1)}, f32[2048,6,16]{0,2,1:T(8,128)}, u32[]{:S(2)}) copy-start(f32[2048,6,16]{0,2,1:T(8,128)} %get-tuple-element.209) | copy-start | bytes 2359300
  471.0 139.1 %reduce-scatter.12.cloned.1.call-start = ((), (), s32[]{:S(2)}) async-start(), calls=%async_computation.14 | async-start | bytes 4718592 | tf_op jit(solution)/shard_map/reduce_scatter | solution.py:303
  506.5 19.7 %copy-start.72 = (bf16[768,1536]{1,0:T(8,128)(2,1)S(1)}, bf16[768,1536]{1,0:T(8,128)(2,1)}, u32[]{:S(2)}) copy-start(bf16[768,1536]{1,0:T(8,128)(2,1)} %all-gather.13.cloned.1.call-done) | copy-start | bytes 7077892
  532.6 84.7 %reduce-scatter.10.cloned.1.call-start = ((), (), s32[]{:S(2)}) async-start(), calls=%async_computation.12 | async-start | bytes 4718592 | tf_op jit(solution)/shard_map/reduce_scatter | solution.py:217
  544.4 11.2 copy-start.71
  566.6 147.3 %reduce-scatter.18.cloned.1.call-start = ((), (), s32[]{:S(2)}) async-start(), calls=%async_computation.17 | async-start | bytes 2506752 | tf_op jit(solution)/shard_map/reduce_scatter | solution.py:335
  572.0 283.6 %reduce-scatter.16.cloned.1.call-start = ((), (), s32[]{:S(2)}) async-start(), calls=%async_computation.16 | async-start | bytes 5013504 | tf_op jit(solution)/shard_map/reduce_scatter | solution.py:334
  582.6 415.1 %reduce-scatter.20.cloned.1.call-start = ((), (), s32[]{:S(2)}) async-start(), calls=%async_computation.18 | async-start | bytes 5013504 | tf_op jit(solution)/shard_map/reduce_scatter | solution.py:336
  592.6 546.5 %reduce-scatter.22.cloned.1.call-start = ((), (), s32[]{:S(2)}) async-start(), calls=%async_computation.19 | async-start | bytes 5013504
  665.4 474.2 %copy-start.75 = (f32[24]{0:T(128)}, f32[24]{0:T(128)S(1)}, u32[]{:S(2)}) copy-start(f32[24]{0:T(128)S(1)} %dynamic-slice.72) | copy-start | bytes 292
  (67 other events, 267.5 us)
Sparse Core Ops, SparseCore 0:
  9.6 14.8 all-gather.16
  27.1 63.8 all-gather.8
  103.4 7.9 all-gather.6
  112.8 13.2 all-gather.10
  128.8 68.1 all-gather.12
  199.6 62.3 all-gather.14
  471.1 12.2 reduce-scatter.13
  532.7 12.2 reduce-scatter.11
  566.7 12.1 reduce-scatter.9
  585.0 128.7 reduce-scatter.17
  719.6 135.9 reduce-scatter.15
  862.0 135.6 reduce-scatter.19
  1003.4 135.5 reduce-scatter.21
